TPU v7x, 128 devices: a whole 4x4x4 slice. The times are simulated.
128 devices in a mesh: row: 8 (over y, x_hi), col: 16 (over z, x_lo, core).
Axes of the slice: x: 4 (x_hi: 2, x_lo: 2; x = x_hi * 2 + x_lo), y: 4, z: 4, core: 2. Of those that a mesh axis runs over, the one named last changes fastest.
Arguments:
- tokens: bfloat16 [128, 512, 256], P('row', 'col'), may hold values from -45 to 45
- cotangent: bfloat16 [128, 512, 256], P('row', 'col'), may hold values from -6 to 6
- gain_one: float32 [256], replicated, may hold values from 0.25 to 1.75
- qkv_weight: bfloat16 [256, 768], replicated, may hold values from -0.375 to 0.375
- proj_weight: bfloat16 [256, 256], replicated, may hold values from -0.375 to 0.375
- rel_bias: float32 [8, 64, 64], replicated, may hold values from -3 to 300
- gain_two: float32 [256], replicated, may hold values from 0.25 to 1.75
- fc_one: bfloat16 [256, 1024], replicated, may hold values from -0.375 to 0.375
- fc_two: bfloat16 [1024, 256], replicated, may hold values from -0.1875 to 0.1875
Outputs:
- output: bfloat16 [128, 512, 256], P('row', 'col')
- grad_tokens: bfloat16 [128, 512, 256], P('row', 'col')
- grad_qkv: float32 [256, 768], replicated
- grad_proj: float32 [256, 256], replicated
- grad_bias: float32 [8, 64, 64], replicated
- grad_fc_one: float32 [256, 1024], replicated
- grad_fc_two: float32 [1024, 256], replicated
- grad_gain_one: float32 [256], replicated
- grad_gain_two: float32 [256], replicated
All inputs are finite; a program needn't handle non-finite values.
Results may differ from a plain program's by a relative error of at most 0.012.
The roundings to bfloat16 on the way count: a program that leaves them out, or rounds other values in their place, can miss the bound.
Values may be sent and summed in bfloat16 or wider, within the bound.
A program may use at most 128 MiB of HBM per device.

v0:
```python
import functools

import jax
import jax.numpy as jnp
from jax import lax
from jax.experimental import pallas as pl
from jax.experimental.pallas import tpu as pltpu
from jax.sharding import PartitionSpec as P

NUM_HEADS = 8
HEAD_DIM = 32
GRID_SIDE = 8
AREA = GRID_SIDE * GRID_SIDE
CHANNELS = 256
MLP_DIM = 1024
WINDOWS = 8
LOCAL = WINDOWS * AREA
PAIRS = 4
LANES = 128
PIECES = 16

EPSILON = 1e-05
ROOT_HALF = 0.7071067811865476
DENSITY = 0.3989422804014327
SCORE_SCALE = HEAD_DIM ** (-0.5)

MESH = pl.DeviceIdType.MESH
BF16 = jnp.bfloat16
F32 = jnp.float32


def low(values):
    return values.astype(BF16)


def wide(values):
    return values.astype(F32)


def dot_nn(a, b):
    return lax.dot_general(a, b, (((1,), (0,)), ((), ())), preferred_element_type=F32)


def dot_nt(a, b):
    return lax.dot_general(a, b, (((1,), (1,)), ((), ())), preferred_element_type=F32)


def dot_tn(a, b):
    return lax.dot_general(a, b, (((0,), (0,)), ((), ())), preferred_element_type=F32)


def norm_forward(values):
    centre = jnp.mean(values, axis=-1, keepdims=True)
    shifted = values - centre
    spread = jnp.mean(shifted * shifted, axis=-1, keepdims=True)
    inverse = lax.rsqrt(spread + EPSILON)
    return (shifted * inverse, inverse)


def norm_backward(upstream, normed, inverse, gain_vec):
    scaled = upstream * gain_vec
    mean_first = jnp.mean(scaled, axis=-1, keepdims=True)
    second = jnp.mean(scaled * normed, axis=-1, keepdims=True)
    return inverse * (scaled - mean_first - normed * second)


def gelu_parts(preact):
    normal_cdf = 0.5 * (1.0 + lax.erf(preact * ROOT_HALF))
    return (preact * normal_cdf, normal_cdf + preact * DENSITY * jnp.exp(-0.5 * preact * preact))


def device_at(x, y, z, core):
    return (y * 2 + x // 2, (z * 2 + x % 2) * 2 + core)


def pack_tile(tile):
    return low(jnp.concatenate([tile[:, :, :LANES], tile[:, :, LANES:]], axis=1))


def fused_kernel(
    tokens_ref, cot_ref, gain_one_ref, wqkv_ref, wproj_ref, bias_ref, gain_two_ref, fc1_ref, fc2_ref,
    out_back, grad_back, gath_a, gath_b, gath_c,
    tok_send, cot_send, out_send, grad_send, tok_recv, cot_recv,
    part_a, part_b, part_c, crecv_a, crecv_b, crecv_c, psend_a, psend_b, psend_c,
    precv_a, precv_b, precv_c, axis_a, axis_b, axis_c,
    mix, x_ref, cot_w, cot_low, n1_ref, n1_low, qkv_ref, att_ref, n2_ref, n2_low, mid_ref,
    acc_ref, gnm_ref, gm_low, gatt_ref, gp_ref, bias_t, gbias, probs_ref, kbig_ref, vbig_ref,
    sems,
):
    row, col = lax.axis_index("row"), lax.axis_index("col")
    core = col % 2
    me = row * GRID_SIDE + col // 2
    x, y, z = (row % 2) * 2 + (col // 2) % 2, row // 2, col // 4
    partner = (row, col + 1 - 2 * core)

    def chip(p):
        return (p // GRID_SIDE, (p % GRID_SIDE) * 2 + core)

    barrier = pltpu.get_barrier_semaphore()

    def greet(i, carry):
        pl.semaphore_signal(barrier, inc=1, device_id=chip(lax.rem(me + i, AREA)), device_id_type=MESH)
        return carry

    lax.fori_loop(1, AREA, greet, 0)
    pl.semaphore_signal(barrier, inc=1, device_id=partner, device_id_type=MESH)

    def exchange_start(send, recv, k):
        def step(i, carry):
            p = lax.rem(me + i, AREA)
            pltpu.make_async_remote_copy(
                src_ref=send.at[p], dst_ref=recv.at[me], send_sem=sems.at[2 * k], recv_sem=sems.at[2 * k + 1],
                device_id=chip(p), device_id_type=MESH,
            ).start()
            return carry

        lax.fori_loop(1, AREA, step, 0)
        recv[me] = send[me]

    def drain(ref, sem):
        pltpu.make_async_copy(ref, ref, sem).wait()

    def exchange_recv(recv, k):
        drain(recv.at[pl.ds(0, AREA - 1)], sems.at[2 * k + 1])

    def exchange_sent(send, k):
        drain(send.at[pl.ds(0, AREA - 1)], sems.at[2 * k])

    def device_a(j):
        return device_at(x, j // 4, j % 4, core)

    def device_b(j):
        return device_at(j % 4, y, j // 4, core)

    def device_c(j):
        return device_at(j % 4, j // 4, z, core)

    parts = (
        (part_a, crecv_a, psend_a, precv_a, axis_a, gath_a, device_a, y * 4 + z,
         lambda t: device_at(t, y, z, core), x, 8),
        (part_b, crecv_b, psend_b, precv_b, axis_b, gath_b, device_b, z * 4 + x,
         lambda t: device_at(x, t, z, core), y, 18),
        (part_c, crecv_c, psend_c, precv_c, axis_c, gath_c, device_c, y * 4 + x,
         lambda t: device_at(x, y, t, core), z, 28),
    )

    def remote(src, dst, k, device):
        return pltpu.make_async_remote_copy(
            src_ref=src, dst_ref=dst, send_sem=sems.at[k], recv_sem=sems.at[k + 1],
            device_id=device, device_id_type=MESH,
        )

    def core_start(g):
        part, crecv, k = g[0], g[1], g[10]
        remote(part.at[1 - core], crecv, k, partner).start()

    def plane_start(g):
        part, crecv, psend, precv, where, mine, k = g[0], g[1], g[2], g[3], g[6], g[7], g[10]
        remote(part.at[1 - core], crecv, k, partner).wait()
        psend[...] = low(wide(part[core]) + wide(crecv[...]))

        def step(i, carry):
            j = lax.rem(mine + i, PIECES)
            remote(psend.at[j], precv.at[mine], k + 2, where(j)).start()
            return carry

        lax.fori_loop(1, PIECES, step, 0)
        precv[mine] = psend[mine]

    def axis_start(g):
        psend, precv, axis, along, place, k = g[2], g[3], g[4], g[8], g[9], g[10]
        drain(psend.at[pl.ds(0, PIECES - 1)], sems.at[k + 2])
        drain(precv.at[pl.ds(0, PIECES - 1)], sems.at[k + 3])
        axis[place] = low(jnp.sum(wide(precv[...]), axis=0))
        for i in range(1, 4):
            remote(axis.at[place], axis.at[place], k + 4, along(lax.rem(place + i, 4))).start()

    def gather_start(g):
        axis, gath, where, mine, k = g[4], g[5], g[6], g[7], g[10]
        drain(axis.at[pl.ds(0, 3)], sems.at[k + 4])
        drain(axis.at[pl.ds(0, 3)], sems.at[k + 5])
        gath[core, mine] = low(jnp.sum(wide(axis[...]), axis=0))

        def step(i, carry):
            j = lax.rem(mine + i, PIECES)
            remote(gath.at[core, mine], gath.at[core, mine], k + 6, where(j)).start()
            return carry

        lax.fori_loop(1, PIECES, step, 0)

    def share_start(g):
        gath, k = g[5], g[10]
        drain(gath.at[core, pl.ds(0, PIECES - 1)], sems.at[k + 6])
        drain(gath.at[core, pl.ds(0, PIECES - 1)], sems.at[k + 7])
        remote(gath.at[core], gath.at[core], k + 8, partner).start()

    def share_wait(g):
        gath, k = g[5], g[10]
        remote(gath.at[core], gath.at[core], k + 8, partner).wait()

    tok_send[...] = pack_tile(wide(tokens_ref[...]).reshape(AREA, WINDOWS, CHANNELS))
    cot_send[...] = pack_tile(wide(cot_ref[...]).reshape(AREA, WINDOWS, CHANNELS))
    pl.semaphore_wait(barrier, AREA)
    exchange_start(tok_send, tok_recv, 0)
    exchange_start(cot_send, cot_recv, 1)

    head_mask = low(wide(
        lax.broadcasted_iota(jnp.int32, (4 * AREA, LANES), 0) // AREA
        == lax.broadcasted_iota(jnp.int32, (4 * AREA, LANES), 1) // HEAD_DIM
    ))
    head_mask_two = jnp.concatenate([head_mask, head_mask], axis=1)
    head_wide = wide(head_mask_two)
    first_rows = lax.broadcasted_iota(jnp.int32, (LANES, LANES), 0) < AREA
    top = low(wide(first_rows))
    bottom = low(1.0 - wide(first_rows))
    for t in range(NUM_HEADS // 2):
        two = jnp.concatenate([bias_ref[2 * t], bias_ref[2 * t + 1]], axis=1)
        bias_t[t // 2, pl.ds((t % 2) * LANES, LANES), :] = jnp.concatenate([two, two], axis=0).T

    gain_one = gain_one_ref[...]
    gain_two = gain_two_ref[...]

    def to_rows(recv, dest):
        tile = wide(recv[...])
        for half in range(2):
            mix[half] = tile[:, 8 * half : 8 * half + 8, :].reshape(LOCAL, LANES)
        for w in range(WINDOWS):
            for half in range(2):
                dest[pl.ds(w * AREA, AREA), pl.ds(half * LANES, LANES)] = mix[half, pl.ds(w, AREA, stride=WINDOWS), :]

    def from_rows(values, send):
        for w in range(WINDOWS):
            for half in range(2):
                mix[half, pl.ds(w, AREA, stride=WINDOWS), :] = values[
                    w * AREA : (w + 1) * AREA, half * LANES : (half + 1) * LANES
                ]
        send[...] = low(jnp.concatenate(
            [mix[0].reshape(AREA, WINDOWS, LANES), mix[1].reshape(AREA, WINDOWS, LANES)], axis=1
        ))

    exchange_recv(tok_recv, 0)
    to_rows(tok_recv, x_ref)
    normed_one, inverse_one = norm_forward(x_ref[...])
    n1_ref[...] = normed_one
    n1_low[...] = low(normed_one * gain_one)
    qkv_ref[...] = low(dot_nn(n1_low[...], wqkv_ref[...]))

    def block(ref, b, part, half):
        return ref[pl.ds(b * LANES, LANES), pl.ds(part * CHANNELS + half * LANES, LANES)]

    def spread(tile):
        return jnp.concatenate([jnp.concatenate([tile[:AREA]] * 4, axis=0) * head_mask,
                                jnp.concatenate([tile[AREA:]] * 4, axis=0) * head_mask], axis=1)

    def diagonal(tile):
        return jnp.concatenate([tile * top, tile * bottom], axis=1)

    def own_window(tile):
        return jnp.where(first_rows, tile[:, :LANES], tile[:, LANES:])

    def own_heads(tile):
        folded = jnp.sum((tile * head_wide).reshape(4, AREA, 2 * LANES), axis=0)
        return jnp.concatenate([folded[:, :LANES], folded[:, LANES:]], axis=0)

    order = [(b, half) for b in range(PAIRS) for half in range(2)]
    for b, half in order:
        slot = 2 * b + half
        kbig_ref[slot] = spread(block(qkv_ref, b, 1, half))
        vbig_ref[slot] = spread(block(qkv_ref, b, 2, half))
        scores = dot_nt(kbig_ref[slot], diagonal(block(qkv_ref, b, 0, half))) * SCORE_SCALE + bias_t[half]
        scores = scores.reshape(4, AREA, LANES)
        raised = jnp.exp(scores - jnp.max(scores, axis=1, keepdims=True))
        probs = raised * (1.0 / jnp.sum(raised, axis=1, keepdims=True))
        probs = probs.reshape(4 * AREA, LANES)
        probs_ref[slot] = probs
        mixed = dot_tn(low(probs), vbig_ref[slot])
        att_ref[pl.ds(b * LANES, LANES), pl.ds(half * LANES, LANES)] = low(own_window(mixed))
    branch = low(dot_nn(att_ref[...], wproj_ref[...]))
    mid_ref[...] = wide(low(x_ref[...] + wide(branch)))

    normed_two, inverse_two = norm_forward(mid_ref[...])
    n2_ref[...] = normed_two
    n2_low[...] = low(normed_two * gain_two)
    exchange_recv(cot_recv, 1)
    to_rows(cot_recv, cot_w)
    cot_low[...] = low(cot_w[...])
    n2_turned = low((normed_two * gain_two)).T
    for j in range(4):
        cut = pl.ds(j * 256, 256)
        preact = dot_nn(n2_low[...], fc1_ref[:, cut])
        activation, slope = gelu_parts(preact)
        activation = low(activation)
        grad_pre = low(dot_nt(cot_low[...], fc2_ref[cut, :]) * slope)
        out_term = dot_nn(activation, fc2_ref[cut, :])
        grad_term = dot_nt(grad_pre, fc1_ref[:, cut])
        if j == 0:
            acc_ref[...] = out_term
            gnm_ref[...] = grad_term
        else:
            acc_ref[...] += out_term
            gnm_ref[...] += grad_term
        block_b = low(dot_tn(activation, cot_low[...]))
        block_a = low(dot_nn(n2_turned, grad_pre))
        for r in range(4):
            for c in range(2):
                part_b[j // 2, ((j % 2) * 4 + r) * 2 + c] = block_b[r * 64 : r * 64 + 64, c * LANES : (c + 1) * LANES]
                part_a[r // 2, (r % 2) * 8 + 2 * j + c] = block_a[r * 64 : r * 64 + 64, c * LANES : (c + 1) * LANES]
    core_start(parts[0])
    core_start(parts[1])
    from_rows(wide(low(mid_ref[...] + acc_ref[...])), out_send)
    exchange_start(out_send, out_back, 2)

    gnm = gnm_ref[...]
    normed_two = n2_ref[...]
    gain_row_two = jnp.sum(gnm * normed_two, axis=0, keepdims=True)
    gm_low[...] = low(cot_w[...] + norm_backward(gnm, normed_two, inverse_two, gain_two))
    gatt_ref[...] = low(dot_nt(gm_low[...], wproj_ref[...]))

    def put(ref, b, part, half, tile):
        ref[pl.ds(b * LANES, LANES), pl.ds(part * CHANNELS + half * LANES, LANES)] = low(tile)

    for n, (b, half) in enumerate(order):
        slot = 2 * b + half
        probs = probs_ref[slot]
        grad_diag = diagonal(block(gatt_ref, b, 0, half))
        grad_probs = dot_nt(vbig_ref[slot], grad_diag)
        put(gp_ref, b, 2, half, own_heads(dot_nn(low(probs), grad_diag)))
        weighted = (probs * grad_probs).reshape(4, AREA, LANES)
        total = jnp.sum(weighted, axis=1, keepdims=True)
        grad_scores = probs * (grad_probs.reshape(4, AREA, LANES) - total).reshape(4 * AREA, LANES)
        if b == 0:
            gbias[half] = grad_scores
        else:
            gbias[half] += grad_scores
        scores_low = low(grad_scores)
        put(gp_ref, b, 0, half, own_window(dot_tn(scores_low, kbig_ref[slot])) * SCORE_SCALE)
        query_diag = diagonal(block(qkv_ref, b, 0, half))
        put(gp_ref, b, 1, half, own_heads(dot_nn(scores_low, query_diag)) * SCORE_SCALE)
        if n == 2:
            plane_start(parts[0])
        if n == 4:
            plane_start(parts[1])

    grad_qkv = low(dot_tn(n1_low[...], gp_ref[...]))
    for h in range(2):
        for r in range(2):
            for c in range(6):
                part_c[h, r * 6 + c, pl.ds(0, 64), :] = grad_qkv[
                    h * 128 + r * 64 : h * 128 + r * 64 + 64, c * LANES : (c + 1) * LANES
                ]
    grad_proj = low(dot_tn(att_ref[...], gm_low[...]))
    for h in range(2):
        for r in range(2):
            for c in range(2):
                part_c[h, 12 + r * 2 + c, pl.ds(0, 64), :] = grad_proj[
                    h * 128 + r * 64 : h * 128 + r * 64 + 64, c * LANES : (c + 1) * LANES
                ]
    grad_normed_in = wide(low(dot_nt(gp_ref[...], wqkv_ref[...])))
    normed_one = n1_ref[...]
    gain_row_one = jnp.sum(grad_normed_in * normed_one, axis=0, keepdims=True)
    gains = jnp.concatenate(
        [gain_row_one[:, :LANES], gain_row_one[:, LANES:], gain_row_two[:, :LANES], gain_row_two[:, LANES:],
         jnp.zeros((4, LANES), F32)], axis=0,
    )
    for h in range(2):
        for t in range(2):
            tile = gbias[h, pl.ds(t * LANES, LANES), :]
            tile = (tile + pltpu.roll(tile, AREA, 1)).T
            for r in range(8):
                part_c[h, t * 8 + r, pl.ds(64, 16), :] = low(
                    jnp.concatenate([tile[8 * r : 8 * r + 8], gains], axis=0)
                )
    core_start(parts[2])
    grad_tokens = wide(gm_low[...]) + norm_backward(grad_normed_in, normed_one, inverse_one, gain_one)
    from_rows(wide(low(grad_tokens)), grad_send)
    exchange_start(grad_send, grad_back, 3)

    plane_start(parts[2])
    axis_start(parts[0])
    axis_start(parts[1])
    axis_start(parts[2])
    gather_start(parts[0])
    gather_start(parts[1])
    gather_start(parts[2])
    share_start(parts[0])
    share_start(parts[1])
    share_start(parts[2])
    exchange_recv(out_back, 2)
    exchange_recv(grad_back, 3)
    exchange_sent(tok_send, 0)
    exchange_sent(cot_send, 1)
    exchange_sent(out_send, 2)
    exchange_sent(grad_send, 3)
    for g in parts:
        share_wait(g)


def final_kernel(
    scale, out_back, grad_back, gath_a, gath_b, gath_c,
    out_ref, gtok_ref, gqkv_ref, gproj_ref, gbias_ref, gfc1_ref, gfc2_ref, gone_ref, gtwo_ref,
):
    for src, dst in ((out_back, out_ref), (grad_back, gtok_ref)):
        tile = wide(src[...])
        joined = jnp.concatenate([tile[:, :8, :], tile[:, 8:, :]], axis=2)
        dst[...] = low(joined.reshape(dst.shape))
    for h in range(2):
        for j in range(PIECES):
            gfc1_ref[pl.ds(h * 128 + (j // 8) * 64, 64), pl.ds((j % 8) * LANES, LANES)] = wide(gath_a[h, j]) * scale
            gfc2_ref[pl.ds(h * 512 + (j // 2) * 64, 64), pl.ds((j % 2) * LANES, LANES)] = wide(gath_b[h, j]) * scale
            tile = wide(gath_c[h, j, pl.ds(0, 64), :]) * scale
            if j < 12:
                gqkv_ref[pl.ds(h * 128 + (j // 6) * 64, 64), pl.ds((j % 6) * LANES, LANES)] = tile
            else:
                t = j - 12
                gproj_ref[pl.ds(h * 128 + (t // 2) * 64, 64), pl.ds((t % 2) * LANES, LANES)] = tile
            extra = wide(gath_c[h, j, pl.ds(64, 16), :])
            bias = extra[:8] * (scale * AREA)
            t, r = j // 8, j % 8
            gbias_ref[4 * h + 2 * t, pl.ds(8 * r, 8), :] = bias[:, :AREA]
            gbias_ref[4 * h + 2 * t + 1, pl.ds(8 * r, 8), :] = bias[:, AREA:]
            if h == 0 and j == 0:
                gone_ref[:, :LANES] = extra[8:9] * scale
                gone_ref[:, LANES:] = extra[9:10] * scale
                gtwo_ref[:, :LANES] = extra[10:11] * scale
                gtwo_ref[:, LANES:] = extra[11:12] * scale


VMEM = pl.BlockSpec(memory_space=pltpu.VMEM)


def body(tokens, cotangent, gain_one, qkv_weight, proj_weight, rel_bias, gain_two, fc_one, fc_two):
    tile_rows, tile_cols, channels = tokens.shape
    total_tokens = tile_rows * tile_cols * lax.axis_size("row") * lax.axis_size("col")
    grad_scale = total_tokens ** (-0.5)

    def shape(*dims, dtype=BF16):
        return jax.ShapeDtypeStruct(dims, dtype)

    def vmem(*dims, dtype=BF16):
        return pltpu.VMEM(dims, dtype)

    swap = (AREA, 16, LANES)
    ab, c = (PIECES, 64, LANES), (PIECES, 80, LANES)
    three = (ab, ab, c)
    swapped = pl.pallas_call(
        fused_kernel,
        out_shape=(shape(*swap), shape(*swap), shape(2, *ab), shape(2, *ab), shape(2, *c)),
        in_specs=[VMEM] * 9,
        out_specs=(VMEM,) * 5,
        scratch_shapes=[
            *[vmem(*swap) for _ in range(6)],
            *[vmem(2, *s) for s in three],
            *[vmem(*s) for s in three],
            *[vmem(*s) for s in three],
            *[vmem(*s) for s in three],
            *[vmem(4, *s[1:]) for s in three],
            vmem(2, LOCAL, LANES, dtype=F32),
            vmem(LOCAL, CHANNELS, dtype=F32),
            vmem(LOCAL, CHANNELS, dtype=F32),
            vmem(LOCAL, CHANNELS),
            vmem(LOCAL, CHANNELS, dtype=F32),
            vmem(LOCAL, CHANNELS),
            vmem(LOCAL, 3 * CHANNELS),
            vmem(LOCAL, CHANNELS),
            vmem(LOCAL, CHANNELS, dtype=F32),
            vmem(LOCAL, CHANNELS),
            vmem(LOCAL, CHANNELS, dtype=F32),
            vmem(LOCAL, CHANNELS, dtype=F32),
            vmem(LOCAL, CHANNELS, dtype=F32),
            vmem(LOCAL, CHANNELS),
            vmem(LOCAL, CHANNELS),
            vmem(LOCAL, 3 * CHANNELS),
            vmem(2, 4 * AREA, LANES, dtype=F32),
            vmem(2, 4 * AREA, LANES, dtype=F32),
            vmem(8, 4 * AREA, LANES, dtype=F32),
            vmem(8, 4 * AREA, 2 * LANES),
            vmem(8, 4 * AREA, 2 * LANES),
            pltpu.SemaphoreType.DMA((38,)),
        ],
        compiler_params=pltpu.CompilerParams(
            collective_id=0, has_side_effects=True, vmem_limit_bytes=48 * 1024 * 1024
        ),
        name="fused",
    )(
        tokens, cotangent, gain_one.reshape(1, -1), qkv_weight, proj_weight, rel_bias,
        gain_two.reshape(1, -1), fc_one, fc_two,
    )
    results = pl.pallas_call(
        functools.partial(final_kernel, grad_scale),
        out_shape=(
            shape(*tokens.shape), shape(*tokens.shape), shape(CHANNELS, 3 * CHANNELS, dtype=F32),
            shape(CHANNELS, CHANNELS, dtype=F32), shape(NUM_HEADS, AREA, AREA, dtype=F32),
            shape(CHANNELS, MLP_DIM, dtype=F32), shape(MLP_DIM, CHANNELS, dtype=F32),
            shape(1, CHANNELS, dtype=F32), shape(1, CHANNELS, dtype=F32),
        ),
        in_specs=[VMEM] * 5,
        out_specs=(VMEM,) * 9,
        compiler_params=pltpu.CompilerParams(vmem_limit_bytes=32 * 1024 * 1024),
        name="finish",
    )(*swapped)
    return (*results[:7], results[7].reshape(-1), results[8].reshape(-1))


def solution(mesh):
    in_specs = (P("row", "col", None), P("row", "col", None), P(), P(), P(), P(), P(), P(), P())
    out_specs = (P("row", "col", None), P("row", "col", None), P(), P(), P(), P(), P(), P(), P())
    return jax.shard_map(body, mesh=mesh, in_specs=in_specs, out_specs=out_specs, check_vma=False)
```

profile of v0, /device:TPU:1, one launch (start us, length us, event | category | flops | bytes accessed | tf_op | source)
XLA Modules:
  0.0 64.6 jit_solution(17993560242316785665)
XLA Ops:
  0.6 0.0 copy-start.8
  0.7 0.0 copy-start.7
  0.7 0.7 %copy-done.8 = f32[256]{0:T(256)S(1)} copy-done((f32[256]{0:T(256)S(1)}, f32[256]{0:T(256)}, u32[]{:S(2)}) %copy-start.8) | copy-done | bytes 1048
  1.3 0.0 copy-done.7
  1.3 0.0 copy-start
  1.3 1.0 %copy-done = bf16[256,1024]{1,0:T(8,128)(2,1)S(1)} copy-done((bf16[256,1024]{1,0:T(8,128)(2,1)S(1)}, bf16[256,1024]{1,0:T(8,128)(2,1)}, u32[]{:S(2)}) %copy-start) | copy-done | bytes 524312
  2.4 0.0 copy-start.1
  2.4 1.0 %copy-done.1 = bf16[1024,256]{1,0:T(8,128)(2,1)S(1)} copy-done((bf16[1024,256]{1,0:T(8,128)(2,1)S(1)}, bf16[1024,256]{1,0:T(8,128)(2,1)}, u32[]{:S(2)}) %copy-start.1) | copy-done | bytes 524312
  3.4 0.0 copy-start.2
  3.4 1.0 %copy-done.2 = bf16[256,768]{1,0:T(8,128)(2,1)S(1)} copy-done((bf16[256,768]{1,0:T(8,128)(2,1)S(1)}, bf16[256,768]{1,0:T(8,128)(2,1)}, u32[]{:S(2)}) %copy-start.2) | copy-done | bytes 393240
  4.4 0.0 copy-start.3
  4.4 0.9 %copy-done.3 = bf16[16,32,256]{2,1,0:T(8,128)(2,1)S(1)} copy-done((bf16[16,32,256]{2,1,0:T(8,128)(2,1)S(1)}, bf16[16,32,256]{2,1,0:T(8,128)(2,1)}, u32[]{:S(2)}) %copy-start.3) | copy-done | bytes 262168
  5.4 0.0 copy-start.4
  5.4 0.9 %copy-done.4 = bf16[16,32,256]{2,1,0:T(8,128)(2,1)S(1)} copy-done((bf16[16,32,256]{2,1,0:T(8,128)(2,1)S(1)}, bf16[16,32,256]{2,1,0:T(8,128)(2,1)}, u32[]{:S(2)}) %copy-start.4) | copy-done | bytes 262168
  6.3 0.0 copy-start.5
  6.3 0.9 %copy-done.5 = f32[8,64,64]{2,1,0:T(8,128)S(1)} copy-done((f32[8,64,64]{2,1,0:T(8,128)S(1)}, f32[8,64,64]{2,1,0:T(8,128)}, u32[]{:S(2)}) %copy-start.5) | copy-done | bytes 131096
  7.3 0.0 copy-start.6
  7.3 0.9 %copy-done.6 = bf16[256,256]{1,0:T(8,128)(2,1)S(1)} copy-done((bf16[256,256]{1,0:T(8,128)(2,1)S(1)}, bf16[256,256]{1,0:T(8,128)(2,1)}, u32[]{:S(2)}) %copy-start.6) | copy-done | bytes 131096
  8.2 54.5 %fused.1 = (bf16[64,16,128]{2,1,0:T(8,128)(2,1)S(1)}, bf16[64,16,128]{2,1,0:T(8,128)(2,1)S(1)}, bf16[2,16,64,128]{3,2,1,0:T(8,128)(2,1)S(1)}, bf16[2,16,64,128]{...) custom-call(bf16[16,32,256]{2,1,0:T(8,128)(2,1)S(1)} %copy-done.3, bf16[16,32,256]{2,1,0:T(8,128)(2,1)S(1)} %copy-done.4, ...), custom_call_target="tpu_custom_call" | custom-call | tf_op jit(solution)/shard_map/fused/pallas_call | solution.py:445
  62.6 2.0 %finish.1 = (bf16[16,32,256]{2,1,0:T(8,128)(2,1)}, bf16[16,32,256]{2,1,0:T(8,128)(2,1)}, f32[256,768]{1,0:T(8,128)}, f32[256,256]{1,0:T(8,128)}, f32[8,64,64]{2,...) custom-call(bf16[64,16,128]{2,1,0:T(8,128)(2,1)S(1)} %get-tuple-element.23.out_ba, ...), custom_call_target="tpu_custom_call" | custom-call | tf_op jit(solution)/shard_map/finish/pallas_call | solution.py:488
Async XLA Ops:
  0.6 0.7 %copy-start.8 = (f32[256]{0:T(256)S(1)}, f32[256]{0:T(256)}, u32[]{:S(2)}) copy-start(f32[256]{0:T(256)} %param.15) | copy-start | bytes 3076
  0.7 0.7 %copy-start.7 = (f32[256]{0:T(256)S(1)}, f32[256]{0:T(256)}, u32[]{:S(2)}) copy-start(f32[256]{0:T(256)} %param.11) | copy-start | bytes 3076
  1.3 1.0 %copy-start = (bf16[256,1024]{1,0:T(8,128)(2,1)S(1)}, bf16[256,1024]{1,0:T(8,128)(2,1)}, u32[]{:S(2)}) copy-start(bf16[256,1024]{1,0:T(8,128)(2,1)} %fc1_ref.1) | copy-start | bytes 1572868
  2.4 1.0 %copy-start.1 = (bf16[1024,256]{1,0:T(8,128)(2,1)S(1)}, bf16[1024,256]{1,0:T(8,128)(2,1)}, u32[]{:S(2)}) copy-start(bf16[1024,256]{1,0:T(8,128)(2,1)} %fc2_ref.1) | copy-start | bytes 1572868
  3.4 1.0 %copy-start.2 = (bf16[256,768]{1,0:T(8,128)(2,1)S(1)}, bf16[256,768]{1,0:T(8,128)(2,1)}, u32[]{:S(2)}) copy-start(bf16[256,768]{1,0:T(8,128)(2,1)} %wqkv_ref.1) | copy-start | bytes 1179652
  4.4 0.9 %copy-start.3 = (bf16[16,32,256]{2,1,0:T(8,128)(2,1)S(1)}, bf16[16,32,256]{2,1,0:T(8,128)(2,1)}, u32[]{:S(2)}) copy-start(bf16[16,32,256]{2,1,0:T(8,128)(2,1)} %tokens_ref.1) | copy-start | bytes 786436
  5.4 0.9 %copy-start.4 = (bf16[16,32,256]{2,1,0:T(8,128)(2,1)S(1)}, bf16[16,32,256]{2,1,0:T(8,128)(2,1)}, u32[]{:S(2)}) copy-start(bf16[16,32,256]{2,1,0:T(8,128)(2,1)} %cot_ref.1) | copy-start | bytes 786436
  6.3 0.9 %copy-start.5 = (f32[8,64,64]{2,1,0:T(8,128)S(1)}, f32[8,64,64]{2,1,0:T(8,128)}, u32[]{:S(2)}) copy-start(f32[8,64,64]{2,1,0:T(8,128)} %bias_ref.1) | copy-start | bytes 393220
  7.3 0.9 %copy-start.6 = (bf16[256,256]{1,0:T(8,128)(2,1)S(1)}, bf16[256,256]{1,0:T(8,128)(2,1)}, u32[]{:S(2)}) copy-start(bf16[256,256]{1,0:T(8,128)(2,1)} %wproj_ref.1) | copy-start | bytes 393220
where the time goes:
time: 65 us; the launch traced here: 64.6 us
  Pallas kernels  56.4 us (87%)
  local copies, waits for them, and re-layouts  7.51 us (12%)
  between operations  0.68 us (1%)
    pallas_call x1, Pallas kernels, body(): pl.pallas_call(fused_kernel, out_shape=(shape(*swap), shape(*swap), shape...  54.5 us
    unnamed x18, local copies, waits for them, and re-layouts  7.51 us
    pallas_call x1, Pallas kernels, body(): pl.pallas_call(functools.partial(final_kernel, grad_scale), out_shape=(sh...  1.96 us

commit v1 on v0

--- a/solution.py
+++ b/solution.py
@@ -78,14 +78,15 @@
 
 
 def fused_kernel(
-    tokens_ref, cot_ref, gain_one_ref, wqkv_ref, wproj_ref, bias_ref, gain_two_ref, fc1_ref, fc2_ref,
+    tokens_in, cot_in, gain_one_in, wqkv_in, wproj_in, bias_in, gain_two_in, fc1_in, fc2_in,
     out_back, grad_back, gath_a, gath_b, gath_c,
     tok_send, cot_send, out_send, grad_send, tok_recv, cot_recv,
     part_a, part_b, part_c, crecv_a, crecv_b, crecv_c, psend_a, psend_b, psend_c,
-    precv_a, precv_b, precv_c, axis_a, axis_b, axis_c,
+    precv_a, precv_b, precv_c, axis_a, axis_b, axis_c, total_a, total_b, total_c,
     mix, x_ref, cot_w, cot_low, n1_ref, n1_low, qkv_ref, att_ref, n2_ref, n2_low, mid_ref,
     acc_ref, gnm_ref, gm_low, gatt_ref, gp_ref, bias_t, gbias, probs_ref, kbig_ref, vbig_ref,
-    sems,
+    tokens_ref, cot_ref, gain_one_ref, wqkv_ref, wproj_ref, bias_ref, gain_two_ref, fc1_ref, fc2_ref,
+    sems, load_sems,
 ):
     row, col = lax.axis_index("row"), lax.axis_index("col")
     core = col % 2
@@ -95,6 +96,17 @@
 
     def chip(p):
         return (p // GRID_SIDE, (p % GRID_SIDE) * 2 + core)
+
+    loads = [
+        pltpu.make_async_copy(src, dst, load_sems.at[n])
+        for n, (src, dst) in enumerate((
+            (tokens_in, tokens_ref), (cot_in, cot_ref), (gain_one_in, gain_one_ref), (wqkv_in, wqkv_ref),
+            (bias_in, bias_ref), (wproj_in, wproj_ref), (gain_two_in, gain_two_ref), (fc1_in, fc1_ref),
+            (fc2_in, fc2_ref),
+        ))
+    ]
+    for load in loads:
+        load.start()
 
     barrier = pltpu.get_barrier_semaphore()
 
@@ -115,7 +127,13 @@
             return carry
 
         lax.fori_loop(1, AREA, step, 0)
-        recv[me] = send[me]
+        if k < 2:
+            recv[me] = send[me]
+        else:
+            own_copy(send, recv, k).start()
+
+    def own_copy(send, recv, k):
+        return pltpu.make_async_copy(send.at[me], recv.at[me], sems.at[42 + k])
 
     def drain(ref, sem):
         pltpu.make_async_copy(ref, ref, sem).wait()
@@ -136,12 +154,12 @@
         return device_at(j % 4, j // 4, z, core)
 
     parts = (
-        (part_a, crecv_a, psend_a, precv_a, axis_a, gath_a, device_a, y * 4 + z,
+        (part_a, crecv_a, psend_a, precv_a, axis_a, total_a, gath_a, device_a, y * 4 + z,
          lambda t: device_at(t, y, z, core), x, 8),
-        (part_b, crecv_b, psend_b, precv_b, axis_b, gath_b, device_b, z * 4 + x,
-         lambda t: device_at(x, t, z, core), y, 18),
-        (part_c, crecv_c, psend_c, precv_c, axis_c, gath_c, device_c, y * 4 + x,
-         lambda t: device_at(x, y, t, core), z, 28),
+        (part_b, crecv_b, psend_b, precv_b, axis_b, total_b, gath_b, device_b, z * 4 + x,
+         lambda t: device_at(x, t, z, core), y, 20),
+        (part_c, crecv_c, psend_c, precv_c, axis_c, total_c, gath_c, device_c, y * 4 + x,
+         lambda t: device_at(x, y, t, core), z, 32),
     )
 
     def remote(src, dst, k, device):
@@ -151,12 +169,12 @@
         )
 
     def core_start(g):
-        part, crecv, k = g[0], g[1], g[10]
+        part, crecv, _, _, _, _, _, _, _, _, _, k = g
         remote(part.at[1 - core], crecv, k, partner).start()
 
     def plane_start(g):
-        part, crecv, psend, precv, where, mine, k = g[0], g[1], g[2], g[3], g[6], g[7], g[10]
-        remote(part.at[1 - core], crecv, k, partner).wait()
+        part, crecv, psend, precv, _, _, _, where, mine, _, _, k = g
+        drain(crecv, sems.at[k + 1])
         psend[...] = low(wide(part[core]) + wide(crecv[...]))
 
         def step(i, carry):
@@ -168,41 +186,53 @@
         precv[mine] = psend[mine]
 
     def axis_start(g):
-        psend, precv, axis, along, place, k = g[2], g[3], g[4], g[8], g[9], g[10]
-        drain(psend.at[pl.ds(0, PIECES - 1)], sems.at[k + 2])
+        _, _, _, precv, axis, _, _, _, _, along, place, k = g
         drain(precv.at[pl.ds(0, PIECES - 1)], sems.at[k + 3])
         axis[place] = low(jnp.sum(wide(precv[...]), axis=0))
         for i in range(1, 4):
             remote(axis.at[place], axis.at[place], k + 4, along(lax.rem(place + i, 4))).start()
 
+    def total_copy(g):
+        _, _, _, _, _, total, gath, _, mine, _, _, k = g
+        return pltpu.make_async_copy(total, gath.at[core, mine], sems.at[k + 10])
+
     def gather_start(g):
-        axis, gath, where, mine, k = g[4], g[5], g[6], g[7], g[10]
-        drain(axis.at[pl.ds(0, 3)], sems.at[k + 4])
+        _, _, _, _, axis, total, gath, where, mine, _, _, k = g
         drain(axis.at[pl.ds(0, 3)], sems.at[k + 5])
-        gath[core, mine] = low(jnp.sum(wide(axis[...]), axis=0))
+        total[...] = low(jnp.sum(wide(axis[...]), axis=0))
 
         def step(i, carry):
             j = lax.rem(mine + i, PIECES)
-            remote(gath.at[core, mine], gath.at[core, mine], k + 6, where(j)).start()
+            remote(total, gath.at[core, mine], k + 6, where(j)).start()
             return carry
 
         lax.fori_loop(1, PIECES, step, 0)
+        total_copy(g).start()
 
     def share_start(g):
-        gath, k = g[5], g[10]
-        drain(gath.at[core, pl.ds(0, PIECES - 1)], sems.at[k + 6])
+        _, _, _, _, _, _, gath, _, _, _, _, k = g
         drain(gath.at[core, pl.ds(0, PIECES - 1)], sems.at[k + 7])
+        total_copy(g).wait()
         remote(gath.at[core], gath.at[core], k + 8, partner).start()
 
     def share_wait(g):
-        gath, k = g[5], g[10]
-        remote(gath.at[core], gath.at[core], k + 8, partner).wait()
-
+        part, crecv, psend, precv, axis, total, gath, _, _, _, _, k = g
+        drain(gath.at[core], sems.at[k + 9])
+        drain(crecv, sems.at[k])
+        drain(psend.at[pl.ds(0, PIECES - 1)], sems.at[k + 2])
+        drain(axis.at[pl.ds(0, 3)], sems.at[k + 4])
+        drain(psend.at[pl.ds(0, PIECES - 1)], sems.at[k + 6])
+        drain(crecv, sems.at[k + 8])
+
+    loads[0].wait()
     tok_send[...] = pack_tile(wide(tokens_ref[...]).reshape(AREA, WINDOWS, CHANNELS))
-    cot_send[...] = pack_tile(wide(cot_ref[...]).reshape(AREA, WINDOWS, CHANNELS))
     pl.semaphore_wait(barrier, AREA)
     exchange_start(tok_send, tok_recv, 0)
+    loads[1].wait()
+    cot_send[...] = pack_tile(wide(cot_ref[...]).reshape(AREA, WINDOWS, CHANNELS))
     exchange_start(cot_send, cot_recv, 1)
+    for load in loads[2:]:
+        load.wait()
 
     head_mask = low(wide(
         lax.broadcasted_iota(jnp.int32, (4 * AREA, LANES), 0) // AREA
@@ -303,10 +333,9 @@
         block_a = low(dot_nn(n2_turned, grad_pre))
         for r in range(4):
             for c in range(2):
-                part_b[j // 2, ((j % 2) * 4 + r) * 2 + c] = block_b[r * 64 : r * 64 + 64, c * LANES : (c + 1) * LANES]
+                part_b[j // 2, ((j % 2) * 4 + r) * 2 + c, pl.ds(0, 64), :] = block_b[r * 64 : r * 64 + 64, c * LANES : (c + 1) * LANES]
                 part_a[r // 2, (r % 2) * 8 + 2 * j + c] = block_a[r * 64 : r * 64 + 64, c * LANES : (c + 1) * LANES]
     core_start(parts[0])
-    core_start(parts[1])
     from_rows(wide(low(mid_ref[...] + acc_ref[...])), out_send)
     exchange_start(out_send, out_back, 2)
 
@@ -314,6 +343,14 @@
     normed_two = n2_ref[...]
     gain_row_two = jnp.sum(gnm * normed_two, axis=0, keepdims=True)
     gm_low[...] = low(cot_w[...] + norm_backward(gnm, normed_two, inverse_two, gain_two))
+    grad_proj = low(dot_tn(att_ref[...], gm_low[...]))
+    for h in range(2):
+        for r in range(8):
+            for c in range(2):
+                part_b[h, r * 2 + c, pl.ds(64, 16), :] = grad_proj[
+                    h * 128 + r * 16 : h * 128 + r * 16 + 16, c * LANES : (c + 1) * LANES
+                ]
+    core_start(parts[1])
     gatt_ref[...] = low(dot_nt(gm_low[...], wproj_ref[...]))
 
     def put(ref, b, part, half, tile):
@@ -343,17 +380,10 @@
 
     grad_qkv = low(dot_tn(n1_low[...], gp_ref[...]))
     for h in range(2):
-        for r in range(2):
+        for r in range(8):
             for c in range(6):
-                part_c[h, r * 6 + c, pl.ds(0, 64), :] = grad_qkv[
-                    h * 128 + r * 64 : h * 128 + r * 64 + 64, c * LANES : (c + 1) * LANES
-                ]
-    grad_proj = low(dot_tn(att_ref[...], gm_low[...]))
-    for h in range(2):
-        for r in range(2):
-            for c in range(2):
-                part_c[h, 12 + r * 2 + c, pl.ds(0, 64), :] = grad_proj[
-                    h * 128 + r * 64 : h * 128 + r * 64 + 64, c * LANES : (c + 1) * LANES
+                part_c[h, r * 2 + c // 3, pl.ds((c % 3) * 16, 16), :] = grad_qkv[
+                    h * 128 + r * 16 : h * 128 + r * 16 + 16, c * LANES : (c + 1) * LANES
                 ]
     grad_normed_in = wide(low(dot_nt(gp_ref[...], wqkv_ref[...])))
     normed_one = n1_ref[...]
@@ -367,15 +397,15 @@
             tile = gbias[h, pl.ds(t * LANES, LANES), :]
             tile = (tile + pltpu.roll(tile, AREA, 1)).T
             for r in range(8):
-                part_c[h, t * 8 + r, pl.ds(64, 16), :] = low(
+                part_c[h, t * 8 + r, pl.ds(48, 16), :] = low(
                     jnp.concatenate([tile[8 * r : 8 * r + 8], gains], axis=0)
                 )
     core_start(parts[2])
     grad_tokens = wide(gm_low[...]) + norm_backward(grad_normed_in, normed_one, inverse_one, gain_one)
     from_rows(wide(low(grad_tokens)), grad_send)
+
+    plane_start(parts[2])
     exchange_start(grad_send, grad_back, 3)
-
-    plane_start(parts[2])
     axis_start(parts[0])
     axis_start(parts[1])
     axis_start(parts[2])
@@ -387,10 +417,10 @@
     share_start(parts[2])
     exchange_recv(out_back, 2)
     exchange_recv(grad_back, 3)
-    exchange_sent(tok_send, 0)
-    exchange_sent(cot_send, 1)
-    exchange_sent(out_send, 2)
-    exchange_sent(grad_send, 3)
+    own_copy(out_send, out_back, 2).wait()
+    own_copy(grad_send, grad_back, 3).wait()
+    for k, send in enumerate((tok_send, cot_send, out_send, grad_send)):
+        exchange_sent(send, k)
     for g in parts:
         share_wait(g)
 
@@ -398,34 +428,64 @@
 def final_kernel(
     scale, out_back, grad_back, gath_a, gath_b, gath_c,
     out_ref, gtok_ref, gqkv_ref, gproj_ref, gbias_ref, gfc1_ref, gfc2_ref, gone_ref, gtwo_ref,
+    *scratch,
 ):
-    for src, dst in ((out_back, out_ref), (grad_back, gtok_ref)):
-        tile = wide(src[...])
+    sources, (out_v, gtok_v, gqkv_v, gproj_v, gbias_v, gfc1_v, gfc2_v, gone_v, gtwo_v) = scratch[:5], scratch[5:14]
+    load_sems, save_sems = scratch[14:]
+    loads = [
+        pltpu.make_async_copy(src, dst, load_sems.at[n])
+        for n, (src, dst) in enumerate(zip((out_back, grad_back, gath_a, gath_b, gath_c), sources))
+    ]
+    for load in loads:
+        load.start()
+    saves = [
+        pltpu.make_async_copy(src, dst, save_sems.at[n])
+        for n, (src, dst) in enumerate((
+            (out_v, out_ref), (gtok_v, gtok_ref), (gfc1_v, gfc1_ref), (gfc2_v, gfc2_ref), (gproj_v, gproj_ref),
+            (gqkv_v, gqkv_ref), (gbias_v, gbias_ref), (gone_v, gone_ref), (gtwo_v, gtwo_ref),
+        ))
+    ]
+    for n, dst in enumerate((out_v, gtok_v)):
+        loads[n].wait()
+        tile = wide(sources[n][...])
         joined = jnp.concatenate([tile[:, :8, :], tile[:, 8:, :]], axis=2)
         dst[...] = low(joined.reshape(dst.shape))
-    for h in range(2):
-        for j in range(PIECES):
-            gfc1_ref[pl.ds(h * 128 + (j // 8) * 64, 64), pl.ds((j % 8) * LANES, LANES)] = wide(gath_a[h, j]) * scale
-            gfc2_ref[pl.ds(h * 512 + (j // 2) * 64, 64), pl.ds((j % 2) * LANES, LANES)] = wide(gath_b[h, j]) * scale
-            tile = wide(gath_c[h, j, pl.ds(0, 64), :]) * scale
-            if j < 12:
-                gqkv_ref[pl.ds(h * 128 + (j // 6) * 64, 64), pl.ds((j % 6) * LANES, LANES)] = tile
-            else:
-                t = j - 12
-                gproj_ref[pl.ds(h * 128 + (t // 2) * 64, 64), pl.ds((t % 2) * LANES, LANES)] = tile
-            extra = wide(gath_c[h, j, pl.ds(64, 16), :])
-            bias = extra[:8] * (scale * AREA)
-            t, r = j // 8, j % 8
-            gbias_ref[4 * h + 2 * t, pl.ds(8 * r, 8), :] = bias[:, :AREA]
-            gbias_ref[4 * h + 2 * t + 1, pl.ds(8 * r, 8), :] = bias[:, AREA:]
-            if h == 0 and j == 0:
-                gone_ref[:, :LANES] = extra[8:9] * scale
-                gone_ref[:, LANES:] = extra[9:10] * scale
-                gtwo_ref[:, :LANES] = extra[10:11] * scale
-                gtwo_ref[:, LANES:] = extra[11:12] * scale
-
-
-VMEM = pl.BlockSpec(memory_space=pltpu.VMEM)
+        saves[n].start()
+    halves = [(h, j) for h in range(2) for j in range(PIECES)]
+    loads[2].wait()
+    for h, j in halves:
+        gfc1_v[pl.ds(h * 128 + (j // 8) * 64, 64), pl.ds((j % 8) * LANES, LANES)] = wide(sources[2][h, j]) * scale
+    saves[2].start()
+    loads[3].wait()
+    for h, j in halves:
+        tile = wide(sources[3][h, j]) * scale
+        gfc2_v[pl.ds(h * 512 + (j // 2) * 64, 64), pl.ds((j % 2) * LANES, LANES)] = tile[:64]
+        gproj_v[pl.ds(h * 128 + (j // 2) * 16, 16), pl.ds((j % 2) * LANES, LANES)] = tile[64:]
+    saves[3].start()
+    saves[4].start()
+    loads[4].wait()
+    for h, j in halves:
+        tile = wide(sources[4][h, j]) * scale
+        for c in range(3):
+            gqkv_v[pl.ds(h * 128 + (j // 2) * 16, 16), pl.ds(((j % 2) * 3 + c) * LANES, LANES)] = (
+                tile[16 * c : 16 * c + 16]
+            )
+        bias = tile[48:56] * AREA
+        t, r = j // 8, j % 8
+        gbias_v[4 * h + 2 * t, pl.ds(8 * r, 8), :] = bias[:, :AREA]
+        gbias_v[4 * h + 2 * t + 1, pl.ds(8 * r, 8), :] = bias[:, AREA:]
+        if h == 0 and j == 0:
+            gone_v[:, :LANES] = tile[56:57]
+            gone_v[:, LANES:] = tile[57:58]
+            gtwo_v[:, :LANES] = tile[58:59]
+            gtwo_v[:, LANES:] = tile[59:60]
+    for save in saves[5:]:
+        save.start()
+    for save in saves:
+        save.wait()
+
+
+HBM = pl.BlockSpec(memory_space=pltpu.HBM)
 
 
 def body(tokens, cotangent, gain_one, qkv_weight, proj_weight, rel_bias, gain_two, fc_one, fc_two):
@@ -440,13 +500,12 @@
         return pltpu.VMEM(dims, dtype)
 
     swap = (AREA, 16, LANES)
-    ab, c = (PIECES, 64, LANES), (PIECES, 80, LANES)
-    three = (ab, ab, c)
+    three = ((PIECES, 64, LANES), (PIECES, 80, LANES), (PIECES, 64, LANES))
     swapped = pl.pallas_call(
         fused_kernel,
-        out_shape=(shape(*swap), shape(*swap), shape(2, *ab), shape(2, *ab), shape(2, *c)),
-        in_specs=[VMEM] * 9,
-        out_specs=(VMEM,) * 5,
+        out_shape=(shape(*swap), shape(*swap), *[shape(2, *s) for s in three]),
+        in_specs=[HBM] * 9,
+        out_specs=(HBM,) * 5,
         scratch_shapes=[
             *[vmem(*swap) for _ in range(6)],
             *[vmem(2, *s) for s in three],
@@ -454,6 +513,7 @@
             *[vmem(*s) for s in three],
             *[vmem(*s) for s in three],
             *[vmem(4, *s[1:]) for s in three],
+            *[vmem(*s[1:]) for s in three],
             vmem(2, LOCAL, LANES, dtype=F32),
             vmem(LOCAL, CHANNELS, dtype=F32),
             vmem(LOCAL, CHANNELS, dtype=F32),
@@ -475,27 +535,43 @@
             vmem(8, 4 * AREA, LANES, dtype=F32),
             vmem(8, 4 * AREA, 2 * LANES),
             vmem(8, 4 * AREA, 2 * LANES),
-            pltpu.SemaphoreType.DMA((38,)),
+            vmem(*tokens.shape),
+            vmem(*cotangent.shape),
+            vmem(1, CHANNELS, dtype=F32),
+            vmem(*qkv_weight.shape),
+            vmem(*proj_weight.shape),
+            vmem(*rel_bias.shape, dtype=F32),
+            vmem(1, CHANNELS, dtype=F32),
+            vmem(*fc_one.shape),
+            vmem(*fc_two.shape),
+            pltpu.SemaphoreType.DMA((46,)),
+            pltpu.SemaphoreType.DMA((9,)),
         ],
         compiler_params=pltpu.CompilerParams(
-            collective_id=0, has_side_effects=True, vmem_limit_bytes=48 * 1024 * 1024
+            collective_id=0, has_side_effects=True, vmem_limit_bytes=60 * 1024 * 1024
         ),
         name="fused",
     )(
         tokens, cotangent, gain_one.reshape(1, -1), qkv_weight, proj_weight, rel_bias,
         gain_two.reshape(1, -1), fc_one, fc_two,
     )
+    outs = (
+        tokens.shape, tokens.shape, qkv_weight.shape, proj_weight.shape, rel_bias.shape, fc_one.shape, fc_two.shape,
+        (1, CHANNELS), (1, CHANNELS),
+    )
+    types = (BF16, BF16, *[F32] * 7)
     results = pl.pallas_call(
         functools.partial(final_kernel, grad_scale),
-        out_shape=(
-            shape(*tokens.shape), shape(*tokens.shape), shape(CHANNELS, 3 * CHANNELS, dtype=F32),
-            shape(CHANNELS, CHANNELS, dtype=F32), shape(NUM_HEADS, AREA, AREA, dtype=F32),
-            shape(CHANNELS, MLP_DIM, dtype=F32), shape(MLP_DIM, CHANNELS, dtype=F32),
-            shape(1, CHANNELS, dtype=F32), shape(1, CHANNELS, dtype=F32),
-        ),
-        in_specs=[VMEM] * 5,
-        out_specs=(VMEM,) * 9,
-        compiler_params=pltpu.CompilerParams(vmem_limit_bytes=32 * 1024 * 1024),
+        out_shape=tuple(shape(*dims, dtype=t) for dims, t in zip(outs, types)),
+        in_specs=[HBM] * 5,
+        out_specs=(HBM,) * 9,
+        scratch_shapes=[
+            vmem(*swap), vmem(*swap), *[vmem(2, *s) for s in three],
+            *[vmem(*dims, dtype=t) for dims, t in zip(outs, types)],
+            pltpu.SemaphoreType.DMA((5,)),
+            pltpu.SemaphoreType.DMA((9,)),
+        ],
+        compiler_params=pltpu.CompilerParams(vmem_limit_bytes=60 * 1024 * 1024),
         name="finish",
     )(*swapped)
     return (*results[:7], results[7].reshape(-1), results[8].reshape(-1))

time: 65 us -> 56.9 us (0.88)
  local copies, waits for them, and re-layouts: 7.51 us -> 0 us
    unnamed x18 -> x0, local copies, waits for them, and re-layouts: 7.51 us -> none
where the time goes in v1:
time: 56.9 us; the launch traced here: 56.7 us
  Pallas kernels  56.1 us (99%)
  between operations  0.65 us (1%)
    pallas_call x1, Pallas kernels, body(): pl.pallas_call(fused_kernel, out_shape=(shape(*swap), shape(*swap), *[sha...  52.9 us
    pallas_call x1, Pallas kernels, body(): pl.pallas_call(functools.partial(final_kernel, grad_scale), out_shape=tup...  3.14 us

profile of v1, /device:TPU:1, one launch (start us, length us, event | category | flops | bytes accessed | tf_op | source)
XLA Modules:
  0.0 56.7 jit_solution(17039215523122899927)
XLA Ops:
  0.6 52.9 %fused.1 = (bf16[64,16,128]{2,1,0:T(8,128)(2,1)}, bf16[64,16,128]{2,1,0:T(8,128)(2,1)}, bf16[2,16,64,128]{3,2,1,0:T(8,128)(2,1)}, bf16[2,16,80,128]{3,2,1,0:T(8,128)(2,1)}, bf16[2,16,64,128]{3,2,1,0:T(8,128)(2,1)}) custom-call(bf16[16,32,256]{2,1,0:T(8,128)(2,1)} %tokens_in.1, bf16[16,32,256]{2,1,0:T(8,128)(2,1)} %cot_in.1, f32[1,256]{1,0:T(1,128)} %bitcast.4, ...), custom_call_target="tpu_custom_call" | custom-call | tf_op jit(solution)/shard_map/fused/pallas_call | solution.py:504
  53.6 3.1 %finish.1 = (bf16[16,32,256]{2,1,0:T(8,128)(2,1)}, bf16[16,32,256]{2,1,0:T(8,128)(2,1)}, f32[256,768]{1,0:T(8,128)}, f32[256,256]{1,0:T(8,128)}, f32[8,64,64]{2,...) custom-call(bf16[64,16,128]{2,1,0:T(8,128)(2,1)} %get-tuple-element.23.out_back, ...), custom_call_target="tpu_custom_call" | custom-call | tf_op jit(solution)/shard_map/finish/pallas_call | solution.py:563

commit v2 on v1

--- a/solution.py
+++ b/solution.py
@@ -69,8 +69,14 @@
     return (preact * normal_cdf, normal_cdf + preact * DENSITY * jnp.exp(-0.5 * preact * preact))
 
 
-def device_at(x, y, z, core):
-    return (y * 2 + x // 2, (z * 2 + x % 2) * 2 + core)
+def hops(steps):
+    return sum(min(d, 4 - d) for d in steps)
+
+
+PLANE_STEPS = sorted(((a, b) for a in range(4) for b in range(4) if a or b), key=hops, reverse=True)
+CHIP_STEPS = sorted(
+    ((a, b, c) for a in range(4) for b in range(4) for c in range(4) if a or b or c), key=hops, reverse=True
+)
 
 
 def pack_tile(tile):
@@ -94,8 +100,16 @@
     x, y, z = (row % 2) * 2 + (col // 2) % 2, row // 2, col // 4
     partner = (row, col + 1 - 2 * core)
 
-    def chip(p):
-        return (p // GRID_SIDE, (p % GRID_SIDE) * 2 + core)
+    xs, ys, zs = ([(v + d) % 4 for d in range(4)] for v in (x, y, z))
+    col_x, row_x = [v % 2 for v in xs], [v // 2 for v in xs]
+
+    def device(dx, dy, dz):
+        return (ys[dy] * 2 + row_x[dx], (zs[dz] * 2 + col_x[dx]) * 2 + core)
+
+    peers = []
+    for steps in CHIP_STEPS:
+        peer_row, peer_col = device(*steps)
+        peers.append((peer_row * GRID_SIDE + peer_col // 2, (peer_row, peer_col)))
 
     loads = [
         pltpu.make_async_copy(src, dst, load_sems.at[n])
@@ -110,23 +124,13 @@
 
     barrier = pltpu.get_barrier_semaphore()
 
-    def greet(i, carry):
-        pl.semaphore_signal(barrier, inc=1, device_id=chip(lax.rem(me + i, AREA)), device_id_type=MESH)
-        return carry
-
-    lax.fori_loop(1, AREA, greet, 0)
+    for _, peer in peers:
+        pl.semaphore_signal(barrier, inc=1, device_id=peer, device_id_type=MESH)
     pl.semaphore_signal(barrier, inc=1, device_id=partner, device_id_type=MESH)
 
     def exchange_start(send, recv, k):
-        def step(i, carry):
-            p = lax.rem(me + i, AREA)
-            pltpu.make_async_remote_copy(
-                src_ref=send.at[p], dst_ref=recv.at[me], send_sem=sems.at[2 * k], recv_sem=sems.at[2 * k + 1],
-                device_id=chip(p), device_id_type=MESH,
-            ).start()
-            return carry
-
-        lax.fori_loop(1, AREA, step, 0)
+        for p, peer in peers:
+            remote(send.at[p], recv.at[me], 2 * k, peer).start()
         if k < 2:
             recv[me] = send[me]
         else:
@@ -144,22 +148,22 @@
     def exchange_sent(send, k):
         drain(send.at[pl.ds(0, AREA - 1)], sems.at[2 * k])
 
-    def device_a(j):
-        return device_at(x, j // 4, j % 4, core)
-
-    def device_b(j):
-        return device_at(j % 4, y, j // 4, core)
-
-    def device_c(j):
-        return device_at(j % 4, j // 4, z, core)
+    def plane_a(a, b):
+        return (ys[a] * 4 + zs[b], device(0, a, b))
+
+    def plane_b(a, b):
+        return (zs[a] * 4 + xs[b], device(b, 0, a))
+
+    def plane_c(a, b):
+        return (ys[a] * 4 + xs[b], device(b, a, 0))
 
     parts = (
-        (part_a, crecv_a, psend_a, precv_a, axis_a, total_a, gath_a, device_a, y * 4 + z,
-         lambda t: device_at(t, y, z, core), x, 8),
-        (part_b, crecv_b, psend_b, precv_b, axis_b, total_b, gath_b, device_b, z * 4 + x,
-         lambda t: device_at(x, t, z, core), y, 20),
-        (part_c, crecv_c, psend_c, precv_c, axis_c, total_c, gath_c, device_c, y * 4 + x,
-         lambda t: device_at(x, y, t, core), z, 32),
+        (part_a, crecv_a, psend_a, precv_a, axis_a, total_a, gath_a, plane_a, y * 4 + z,
+         lambda d: device(d, 0, 0), x, 8),
+        (part_b, crecv_b, psend_b, precv_b, axis_b, total_b, gath_b, plane_b, z * 4 + x,
+         lambda d: device(0, d, 0), y, 20),
+        (part_c, crecv_c, psend_c, precv_c, axis_c, total_c, gath_c, plane_c, y * 4 + x,
+         lambda d: device(0, 0, d), z, 32),
     )
 
     def remote(src, dst, k, device):
@@ -177,12 +181,9 @@
         drain(crecv, sems.at[k + 1])
         psend[...] = low(wide(part[core]) + wide(crecv[...]))
 
-        def step(i, carry):
-            j = lax.rem(mine + i, PIECES)
-            remote(psend.at[j], precv.at[mine], k + 2, where(j)).start()
-            return carry
-
-        lax.fori_loop(1, PIECES, step, 0)
+        for steps in PLANE_STEPS:
+            j, peer = where(*steps)
+            remote(psend.at[j], precv.at[mine], k + 2, peer).start()
         precv[mine] = psend[mine]
 
     def axis_start(g):
@@ -190,7 +191,7 @@
         drain(precv.at[pl.ds(0, PIECES - 1)], sems.at[k + 3])
         axis[place] = low(jnp.sum(wide(precv[...]), axis=0))
         for i in range(1, 4):
-            remote(axis.at[place], axis.at[place], k + 4, along(lax.rem(place + i, 4))).start()
+            remote(axis.at[place], axis.at[place], k + 4, along(i)).start()
 
     def total_copy(g):
         _, _, _, _, _, total, gath, _, mine, _, _, k = g
@@ -201,12 +202,8 @@
         drain(axis.at[pl.ds(0, 3)], sems.at[k + 5])
         total[...] = low(jnp.sum(wide(axis[...]), axis=0))
 
-        def step(i, carry):
-            j = lax.rem(mine + i, PIECES)
-            remote(total, gath.at[core, mine], k + 6, where(j)).start()
-            return carry
-
-        lax.fori_loop(1, PIECES, step, 0)
+        for steps in PLANE_STEPS:
+            remote(total, gath.at[core, mine], k + 6, where(*steps)[1]).start()
         total_copy(g).start()
 
     def share_start(g):
@@ -228,9 +225,6 @@
     tok_send[...] = pack_tile(wide(tokens_ref[...]).reshape(AREA, WINDOWS, CHANNELS))
     pl.semaphore_wait(barrier, AREA)
     exchange_start(tok_send, tok_recv, 0)
-    loads[1].wait()
-    cot_send[...] = pack_tile(wide(cot_ref[...]).reshape(AREA, WINDOWS, CHANNELS))
-    exchange_start(cot_send, cot_recv, 1)
     for load in loads[2:]:
         load.wait()
 
@@ -267,6 +261,10 @@
         send[...] = low(jnp.concatenate(
             [mix[0].reshape(AREA, WINDOWS, LANES), mix[1].reshape(AREA, WINDOWS, LANES)], axis=1
         ))
+
+    loads[1].wait()
+    cot_send[...] = pack_tile(wide(cot_ref[...]).reshape(AREA, WINDOWS, CHANNELS))
+    exchange_start(cot_send, cot_recv, 1)
 
     exchange_recv(tok_recv, 0)
     to_rows(tok_recv, x_ref)
@@ -436,7 +434,7 @@
         pltpu.make_async_copy(src, dst, load_sems.at[n])
         for n, (src, dst) in enumerate(zip((out_back, grad_back, gath_a, gath_b, gath_c), sources))
     ]
-    for load in loads:
+    for load in loads[2:] + loads[:2]:
         load.start()
     saves = [
         pltpu.make_async_copy(src, dst, save_sems.at[n])
@@ -445,12 +443,6 @@
             (gqkv_v, gqkv_ref), (gbias_v, gbias_ref), (gone_v, gone_ref), (gtwo_v, gtwo_ref),
         ))
     ]
-    for n, dst in enumerate((out_v, gtok_v)):
-        loads[n].wait()
-        tile = wide(sources[n][...])
-        joined = jnp.concatenate([tile[:, :8, :], tile[:, 8:, :]], axis=2)
-        dst[...] = low(joined.reshape(dst.shape))
-        saves[n].start()
     halves = [(h, j) for h in range(2) for j in range(PIECES)]
     loads[2].wait()
     for h, j in halves:
@@ -481,6 +473,12 @@
             gtwo_v[:, LANES:] = tile[59:60]
     for save in saves[5:]:
         save.start()
+    for n, dst in enumerate((out_v, gtok_v)):
+        loads[n].wait()
+        tile = wide(sources[n][...])
+        joined = jnp.concatenate([tile[:, :8, :], tile[:, 8:, :]], axis=2)
+        dst[...] = low(joined.reshape(dst.shape))
+        saves[n].start()
     for save in saves:
         save.wait()
 

time: 56.9 us -> 54.1 us (0.951)
  Pallas kernels: 56.1 us -> 53.3 us
    pallas_call x1, Pallas kernels: 52.9 us -> 50.2 us  [body(): pl.pallas_call(fused_kernel, out_shape=(shape(*swap), shape(*swap), *[sha...]
where the time goes in v2:
time: 54.1 us; the launch traced here: 54 us
  Pallas kernels  53.3 us (99%)
  between operations  0.65 us (1%)
    pallas_call x1, Pallas kernels, body(): pl.pallas_call(fused_kernel, out_shape=(shape(*swap), shape(*swap), *[sha...  50.2 us
    pallas_call x1, Pallas kernels, body(): pl.pallas_call(functools.partial(final_kernel, grad_scale), out_shape=tup...  3.16 us

profile of v2, /device:TPU:1, one launch (start us, length us, event | category | flops | bytes accessed | tf_op | source)
XLA Modules:
  0.0 54.0 jit_solution(1335603715551053169)
XLA Ops:
  0.6 50.2 %fused.1 = (bf16[64,16,128]{2,1,0:T(8,128)(2,1)}, bf16[64,16,128]{2,1,0:T(8,128)(2,1)}, bf16[2,16,64,128]{3,2,1,0:T(8,128)(2,1)}, bf16[2,16,80,128]{3,2,1,0:T(8,128)(2,1)}, bf16[2,16,64,128]{3,2,1,0:T(8,128)(2,1)}) custom-call(bf16[16,32,256]{2,1,0:T(8,128)(2,1)} %tokens_in.1, bf16[16,32,256]{2,1,0:T(8,128)(2,1)} %cot_in.1, f32[1,256]{1,0:T(1,128)} %bitcast.4, ...), custom_call_target="tpu_custom_call" | custom-call | tf_op jit(solution)/shard_map/fused/pallas_call | solution.py:502
  50.8 3.2 %finish.1 = (bf16[16,32,256]{2,1,0:T(8,128)(2,1)}, bf16[16,32,256]{2,1,0:T(8,128)(2,1)}, f32[256,768]{1,0:T(8,128)}, f32[256,256]{1,0:T(8,128)}, f32[8,64,64]{2,...) custom-call(bf16[64,16,128]{2,1,0:T(8,128)(2,1)} %get-tuple-element.23.out_back, ...), custom_call_target="tpu_custom_call" | custom-call | tf_op jit(solution)/shard_map/finish/pallas_call | solution.py:561

commit v3 on v2

--- a/solution.py
+++ b/solution.py
@@ -111,6 +111,12 @@
         peer_row, peer_col = device(*steps)
         peers.append((peer_row * GRID_SIDE + peer_col // 2, (peer_row, peer_col)))
 
+    barrier = pltpu.get_barrier_semaphore()
+
+    for _, peer in peers:
+        pl.semaphore_signal(barrier, inc=1, device_id=peer, device_id_type=MESH)
+    pl.semaphore_signal(barrier, inc=1, device_id=partner, device_id_type=MESH)
+
     loads = [
         pltpu.make_async_copy(src, dst, load_sems.at[n])
         for n, (src, dst) in enumerate((
@@ -122,12 +128,6 @@
     for load in loads:
         load.start()
 
-    barrier = pltpu.get_barrier_semaphore()
-
-    for _, peer in peers:
-        pl.semaphore_signal(barrier, inc=1, device_id=peer, device_id_type=MESH)
-    pl.semaphore_signal(barrier, inc=1, device_id=partner, device_id_type=MESH)
-
     def exchange_start(send, recv, k):
         for p, peer in peers:
             remote(send.at[p], recv.at[me], 2 * k, peer).start()
@@ -179,12 +179,11 @@
     def plane_start(g):
         part, crecv, psend, precv, _, _, _, where, mine, _, _, k = g
         drain(crecv, sems.at[k + 1])
-        psend[...] = low(wide(part[core]) + wide(crecv[...]))
-
         for steps in PLANE_STEPS:
             j, peer = where(*steps)
+            psend[j] = low(wide(part[core, j]) + wide(crecv[j]))
             remote(psend.at[j], precv.at[mine], k + 2, peer).start()
-        precv[mine] = psend[mine]
+        precv[mine] = low(wide(part[core, mine]) + wide(crecv[mine]))
 
     def axis_start(g):
         _, _, _, precv, axis, _, _, _, _, along, place, k = g
@@ -193,28 +192,26 @@
         for i in range(1, 4):
             remote(axis.at[place], axis.at[place], k + 4, along(i)).start()
 
-    def total_copy(g):
-        _, _, _, _, _, total, gath, _, mine, _, _, k = g
-        return pltpu.make_async_copy(total, gath.at[core, mine], sems.at[k + 10])
-
     def gather_start(g):
-        _, _, _, _, axis, total, gath, where, mine, _, _, k = g
+        _, _, _, _, axis, held, _, where, mine, _, _, k = g
         drain(axis.at[pl.ds(0, 3)], sems.at[k + 5])
-        total[...] = low(jnp.sum(wide(axis[...]), axis=0))
-
+        held[mine] = low(jnp.sum(wide(axis[...]), axis=0))
         for steps in PLANE_STEPS:
-            remote(total, gath.at[core, mine], k + 6, where(*steps)[1]).start()
-        total_copy(g).start()
+            remote(held.at[mine], held.at[mine], k + 6, where(*steps)[1]).start()
+
+    def held_copy(g):
+        return pltpu.make_async_copy(g[5], g[6].at[core], sems.at[g[-1] + 10])
 
     def share_start(g):
-        _, _, _, _, _, _, gath, _, _, _, _, k = g
-        drain(gath.at[core, pl.ds(0, PIECES - 1)], sems.at[k + 7])
-        total_copy(g).wait()
-        remote(gath.at[core], gath.at[core], k + 8, partner).start()
+        _, _, _, _, _, held, gath, _, _, _, _, k = g
+        drain(held.at[pl.ds(0, PIECES - 1)], sems.at[k + 7])
+        remote(held, gath.at[core], k + 8, partner).start()
+        held_copy(g).start()
 
     def share_wait(g):
         part, crecv, psend, precv, axis, total, gath, _, _, _, _, k = g
         drain(gath.at[core], sems.at[k + 9])
+        held_copy(g).wait()
         drain(crecv, sems.at[k])
         drain(psend.at[pl.ds(0, PIECES - 1)], sems.at[k + 2])
         drain(axis.at[pl.ds(0, 3)], sems.at[k + 4])
@@ -511,7 +508,7 @@
             *[vmem(*s) for s in three],
             *[vmem(*s) for s in three],
             *[vmem(4, *s[1:]) for s in three],
-            *[vmem(*s[1:]) for s in three],
+            *[vmem(*s) for s in three],
             vmem(2, LOCAL, LANES, dtype=F32),
             vmem(LOCAL, CHANNELS, dtype=F32),
             vmem(LOCAL, CHANNELS, dtype=F32),

time: 54.1 us -> 53.6 us (level)
  no operation moved by 1% of the time
where the time goes in v3:
time: 53.6 us; the launch traced here: 53.5 us
  Pallas kernels  52.8 us (99%)
  between operations  0.65 us (1%)
    pallas_call x1, Pallas kernels, body(): pl.pallas_call(fused_kernel, out_shape=(shape(*swap), shape(*swap), *[sha...  49.6 us
    pallas_call x1, Pallas kernels, body(): pl.pallas_call(functools.partial(final_kernel, grad_scale), out_shape=tup...  3.16 us

profile of v3, /device:TPU:1, one launch (start us, length us, event | category | flops | bytes accessed | tf_op | source)
XLA Modules:
  0.0 53.5 jit_solution(10039035409326475192)
XLA Ops:
  0.6 49.6 %fused.1 = (bf16[64,16,128]{2,1,0:T(8,128)(2,1)}, bf16[64,16,128]{2,1,0:T(8,128)(2,1)}, bf16[2,16,64,128]{3,2,1,0:T(8,128)(2,1)}, bf16[2,16,80,128]{3,2,1,0:T(8,128)(2,1)}, bf16[2,16,64,128]{3,2,1,0:T(8,128)(2,1)}) custom-call(bf16[16,32,256]{2,1,0:T(8,128)(2,1)} %tokens_in.1, bf16[16,32,256]{2,1,0:T(8,128)(2,1)} %cot_in.1, f32[1,256]{1,0:T(1,128)} %bitcast.4, ...), custom_call_target="tpu_custom_call" | custom-call | tf_op jit(solution)/shard_map/fused/pallas_call | solution.py:499
  50.3 3.2 %finish.1 = (bf16[16,32,256]{2,1,0:T(8,128)(2,1)}, bf16[16,32,256]{2,1,0:T(8,128)(2,1)}, f32[256,768]{1,0:T(8,128)}, f32[256,256]{1,0:T(8,128)}, f32[8,64,64]{2,...) custom-call(bf16[64,16,128]{2,1,0:T(8,128)(2,1)} %get-tuple-element.23.out_back, ...), custom_call_target="tpu_custom_call" | custom-call | tf_op jit(solution)/shard_map/finish/pallas_call | solution.py:558
